TPU v7x, 768 devices: a whole 4x8x12 slice. The times are simulated.
768 devices in a mesh: dp: 128 (over y, x, z_hi), tensor: 6 (over z_lo, core).
Axes of the slice: x: 4, y: 8, z: 12 (z_hi: 4, z_lo: 3; z = z_hi * 3 + z_lo), core: 2. Of those that a mesh axis runs over, the one named last changes fastest.
Arguments:
- teacher_in: bfloat16 [16384, 1920], P('dp', 'tensor'), may hold values from -3 to 3
- norm_gain: float32 [1920], replicated, may hold values from 0.1 to 1.9
- fc1_weight: bfloat16 [1920, 7680], P(None, 'tensor'), may hold values from -0.125 to 0.125
- fc2_weight: bfloat16 [7680, 1920], P('tensor'), may hold values from -0.0625 to 0.0625
- layer_scale: float32 [1920], P('tensor'), may hold values from 0.5 to 2
- route: int32 [16384], P('dp'), may hold values from 0 to 127, as said below
- student_feat: bfloat16 [16384, 1280], P('dp'), may hold values from -24 to 24
- adaptor_weight: bfloat16 [1280, 1920], P(None, 'tensor'), may hold values from -0.15625 to 0.15625
Outputs:
- adaptor_grad: float32 [1280, 1920], P('dp', 'tensor')
Inputs may be any that keep to these rules, and one draw needn't show every extreme that they name: `route`: within each aligned block of 128 tokens every value appears exactly 128 // 128 times.
All inputs are finite; a program needn't handle non-finite values.
Results may differ from a plain program's by a relative error of at most 0.0053.
Values may be sent and summed in bfloat16 or wider, within the bound.
A program may use at most 32 MiB of HBM per device.

v0:
```python
import math

import jax
import jax.numpy as jnp
from jax import lax
from jax.sharding import PartitionSpec as P


def local(
    teacher_in, norm_gain, fc1_weight, fc2_weight, layer_scale, route, student_feat, adaptor_weight
):
    row_count = teacher_in.shape[0]
    dp_devices = lax.axis_size("dp")
    sort_keys = route * row_count + jnp.arange(row_count, dtype=jnp.int32)
    arrival = jnp.argsort(sort_keys)
    gathered = lax.all_gather(teacher_in, "tensor", axis=1, tiled=True)
    widened = gathered.astype(jnp.float32)
    normed = (
        widened * lax.rsqrt(jnp.mean(widened * widened, axis=1, keepdims=True) + 1e-06) * norm_gain
    ).astype(jnp.bfloat16)
    hidden = jax.nn.gelu(
        jnp.dot(normed, fc1_weight, preferred_element_type=jnp.float32), approximate=False
    ).astype(jnp.bfloat16)
    partial_value = jnp.dot(hidden, fc2_weight, preferred_element_type=jnp.float32)
    mlp_output = lax.psum_scatter(partial_value, "tensor", scatter_dimension=1, tiled=True)
    feature = (teacher_in.astype(jnp.float32) + layer_scale * mlp_output).astype(jnp.bfloat16)
    target = lax.all_to_all(feature[arrival], "dp", split_axis=0, concat_axis=0, tiled=True)
    predicted = jnp.dot(student_feat, adaptor_weight, preferred_element_type=jnp.float32)
    target_wide = target.astype(jnp.float32)
    agreement, target_sq, predict_sq = lax.psum(
        (
            jnp.sum(target_wide * predicted, axis=1),
            jnp.sum(target_wide * target_wide, axis=1),
            jnp.sum(predicted * predicted, axis=1),
        ),
        "tensor",
    )
    target_norm = jnp.sqrt(target_sq + 1e-06)
    predict_norm = jnp.sqrt(predict_sq + 1e-06)
    cosine = agreement / (target_norm * predict_norm)
    teacher_width = adaptor_weight.shape[1] * lax.axis_size("tensor")
    loss_scale = teacher_width / math.sqrt(row_count * dp_devices)
    upstream = (
        -loss_scale
        * (
            target_wide / (target_norm * predict_norm)[:, None]
            - (cosine / (predict_norm * predict_norm))[:, None] * predicted
        )
    ).astype(jnp.bfloat16)
    return lax.psum_scatter(
        lax.dot_general(
            student_feat, upstream, (((0,), (0,)), ((), ())), preferred_element_type=jnp.float32
        ),
        "dp",
        scatter_dimension=0,
        tiled=True,
    )


def solution(mesh):
    placed = (
        P("dp", "tensor"),
        P(),
        P(None, "tensor"),
        P("tensor", None),
        P("tensor"),
        P("dp"),
        P("dp", None),
        P(None, "tensor"),
    )
    return jax.shard_map(
        local, mesh=mesh, in_specs=placed, out_specs=P("dp", "tensor"), check_vma=False
    )
```

profile of v0, /device:TPU:32, one launch (start us, length us, event | category | flops | bytes accessed | tf_op | source)
XLA Modules:
  0.0 1646.3 jit_solution(17228525709083844908)
XLA Ops:
  6.5 0.0 copy-start
  6.5 0.0 reduce-scatter.3.cloned.1.call-start
  6.5 13.2 all_gather.3
  19.8 0.3 fusion
  20.0 0.0 copy-start.4
  20.1 0.0 copy-start.2
  20.1 0.0 copy-start.3
  20.1 0.0 copy-start.1
  20.1 8.8 fusion.18
  28.9 0.0 reduce-scatter.3.cloned.1.call-update
  29.0 0.0 all-reduce.4.cloned.1.call-start
  29.0 0.0 copy-done.4
  29.0 2.5 sort.17
  31.6 37.5 %reduce-scatter.3.cloned.1.call-done = f32[128,320]{0,1:T(8,128)} async-done(((f32[128,1920]{0,1:T(8,128)}), f32[128,320]{0,1:T(8,128)}) %reduce-scatter.3.cloned.1.call-update) | async-done | bytes 163856 | tf_op jit(solution)/shard_map/reduce_scatter | solution.py:25
  69.1 0.0 copy-done.2
  69.1 0.0 copy-done.3
  69.1 1.0 add_convert_fusion
  70.2 0.1 copy.12
  70.3 0.9 gather_fusion
  71.1 0.5 broadcast.34
  71.7 0.7 reduce
  72.3 0.1 reshape.29
  72.4 33.0 %all_to_all.9 = bf16[128,2,160]{2,1,0:T(2,128)(2,1)S(1)} all-to-all(bf16[128,2,160]{2,1,0:T(2,128)(2,1)S(1)} %reshape.29), channel_id=1, replica_groups=mesh['dp'=128,'tensor'=6] {'dp'}, dimensions={0} | all-to-all | bytes 163840 | tf_op jit(solution)/shard_map/all_to_all | solution.py:27
  105.4 0.2 reshape.30
  105.6 0.2 copy.14
  105.8 0.0 copy-done
  105.8 0.0 copy-done.1
  105.8 0.4 multiply_reduce_fusion
  106.2 10.5 all-reduce.1
  116.7 1.6 convolution_bitcast_fusion
  118.3 0.0 all-reduce.4.cloned.1.call-update
  118.3 1.3 dynamic-slice
  120.2 1517.4 %all-reduce.4.cloned.1.call-done = f32[1280,320]{0,1:T(8,128)} async-done(((f32[1280,320]{0,1:T(8,128)}), f32[1280,320]{0,1:T(8,128)}) %all-reduce.4.cloned.1.call-update) | async-done | bytes 1638416
  1637.6 1.1 constant_dynamic-slice_fusion
  1638.7 0.7 copy.15
  (6 shorter events, 0.0 us)
Async XLA Ops:
  6.5 99.3 %copy-start = (bf16[1280,320]{0,1:T(8,128)(2,1)S(1)}, bf16[1280,320]{0,1:T(8,128)(2,1)}, u32[]{:S(2)}) copy-start(bf16[1280,320]{0,1:T(8,128)(2,1)} %param.15) | copy-start | bytes 2457604
  6.5 62.6 %reduce-scatter.3.cloned.1.call-start = ((), (), s32[]{:S(2)}) async-start(), calls=%async_computation.2 | async-start | bytes 1146880 | tf_op jit(solution)/shard_map/reduce_scatter | solution.py:25
  20.0 9.0 copy-start.4
  20.1 49.1 %copy-start.2 = (bf16[128,320]{0,1:T(8,128)(2,1)S(1)}, bf16[128,320]{0,1:T(8,128)(2,1)}, u32[]{:S(2)}) copy-start(bf16[128,320]{0,1:T(8,128)(2,1)} %param.8) | copy-start | bytes 245764
  20.1 49.1 %copy-start.3 = (f32[320]{0:T(512)S(1)}, f32[320]{0:T(512)}, u32[]{:S(2)}) copy-start(f32[320]{0:T(512)} %param.12) | copy-start | bytes 3844
  20.1 85.7 %copy-start.1 = (bf16[128,1280]{1,0:T(8,128)(2,1)S(1)}, bf16[128,1280]{1,0:T(8,128)(2,1)}, u32[]{:S(2)}) copy-start(bf16[128,1280]{1,0:T(8,128)(2,1)} %param.14) | copy-start | bytes 983044
  29.0 1608.7 %all-reduce.4.cloned.1.call-start = ((), (), s32[]{:S(2)}) async-start(), calls=%async_computation.3 | async-start | bytes 3276800
Sparse Core Ops, SparseCore 0:
  29.1 39.9 reduce-scatter.2
  118.4 1519.1 all-reduce.3
where the time goes:
time: 1650 us
  waiting for transfers between devices  1550 us (94%)
  blocking collectives  56.7 us (3%)
    unnamed x3, waiting for transfers between devices  1520 us
    reduce_scatter x1, waiting for transfers between devices, local(): lax.psum_scatter(partial_value, 'tensor', scatter_dimension=1, tiled=True)  37.5 us
  transfers between devices with their start and end apart: 2, of which 2 were waited for; matrix products, arithmetic and copies ran while one was open for 0% of the time, Pallas kernels for 0%

commit v1 on v0

--- a/solution.py
+++ b/solution.py
@@ -1,9 +1,208 @@
+import functools
 import math
 
 import jax
 import jax.numpy as jnp
 from jax import lax
+from jax.experimental import pallas as pl
+from jax.experimental.pallas import tpu as pltpu
 from jax.sharding import PartitionSpec as P
+
+MESH = pl.DeviceIdType.MESH
+NY, NX, NZ = 8, 4, 4
+LANES = 128
+
+
+def round_up(value, unit):
+    return -(-value // unit) * unit
+
+
+def place(y, x, z):
+    return (y * NX + x) * NZ + z
+
+
+def dp_peers(y, x, z):
+    peers = [place(y, lax.rem(x + k, NX), z) for k in (1, NX - 1)]
+    peers += [place(lax.rem(y + k, NY), x, z) for k in range(1, NY)]
+    peers += [place(y, x, lax.rem(z + k, NZ)) for k in range(1, NZ)]
+    return peers
+
+
+def nearest_first(count):
+    order = []
+    for k in range(1, count // 2 + 1):
+        order += [k] if 2 * k == count else [k, count - k]
+    return order
+
+
+def grad_kernel(st_ref, u_ref, out_ref, s1, r1, s2, r2, own, ys, yr, yown, zs, zr, send, recv):
+    me = lax.axis_index("dp")
+    z = lax.rem(me, NZ)
+    x = lax.rem(lax.div(me, NZ), NX)
+    y = lax.div(me, NZ * NX)
+    right, left, across = (lax.rem(x + k, NX) for k in (1, 3, 2))
+    rows = out_ref.shape[0]
+    span = NZ * rows
+    pad = round_up(span, 16)
+    tile = zs.shape[2]
+    full = NY * span
+    chunks = [(0, full, 128), (128, full, 128), (256, full // 2, 64)]
+
+    barrier = pltpu.get_barrier_semaphore()
+    peers = dp_peers(y, x, z)
+    for peer in peers:
+        pl.semaphore_signal(barrier, inc=1, device_id={"dp": peer}, device_id_type=MESH)
+    pl.semaphore_wait(barrier, len(peers))
+
+    def copy(c, slot, src, dst, peer):
+        return pltpu.make_async_remote_copy(
+            src_ref=src, dst_ref=dst, send_sem=send.at[c, slot], recv_sem=recv.at[c, slot],
+            device_id={"dp": peer}, device_id_type=MESH,
+        )
+
+    started = []
+
+    def product(c, block):
+        start, height, width = chunks[c]
+        cols = u_ref[:, start : start + width]
+        if width == LANES:
+            return jnp.dot(st_ref[block], cols, preferred_element_type=jnp.float32)
+        zeros = jnp.zeros_like(cols)
+        low = jnp.concatenate([cols, zeros], axis=1)
+        high = jnp.concatenate([zeros, cols], axis=1)
+        return jnp.dot(
+            st_ref[block, pl.ds(0, height)], low, preferred_element_type=jnp.float32
+        ) + jnp.dot(st_ref[block, pl.ds(height, height)], high, preferred_element_type=jnp.float32)
+
+    def halves(c):
+        half = chunks[c][1] // 2
+        return pl.ds(0, half), pl.ds(half, half)
+
+    def first_x(c):
+        height = chunks[c][1]
+        s1[c, pl.ds(0, height)] = product(c, across).astype(jnp.bfloat16)
+        out = []
+        for side, (part, peer) in enumerate(zip(halves(c), (right, left))):
+            out.append(copy(c, side, s1.at[c, part], r1.at[c, part], place(y, peer, z)))
+            out[-1].start()
+        return out
+
+    def second_x(c, before):
+        height = chunks[c][1]
+        out = []
+        for side, (part, peer) in enumerate(zip(halves(c), (right, left))):
+            value = product(c, peer)
+            s2[c, side, pl.ds(0, height)] = value.astype(jnp.bfloat16)
+            before[side].wait_recv()
+            s2[c, side, part] = (
+                value[part.start : part.start + part.size] + r1[c, part].astype(jnp.float32)
+            ).astype(jnp.bfloat16)
+            out.append(
+                copy(
+                    c, 2 + side, s2.at[c, side, pl.ds(0, height)], r2.at[c, side, pl.ds(0, height)],
+                    place(y, peer, z),
+                )
+            )
+            out[-1].start()
+        own[c, pl.ds(0, height)] = product(c, x)
+        return out
+
+    def send_y(c, before):
+        height, width = chunks[c][1:]
+        value = own[c, pl.ds(0, height)]
+        for side in range(2):
+            before[side].wait_recv()
+            value += r2[c, side, pl.ds(0, height)].astype(jnp.float32)
+        if width == LANES:
+            value = value.reshape(NY, span, LANES)
+        else:
+            value = value.reshape(NY // 2, span, LANES)
+            rolled = pltpu.roll(value.reshape(height, LANES), 64, 1).reshape(NY // 2, span, LANES)
+            value = jnp.concatenate([value, rolled], axis=0)
+        yown[c] = value
+        ys[c] = jnp.concatenate(
+            [value, jnp.zeros((NY, pad - span, LANES), jnp.float32)], axis=1
+        ).astype(jnp.bfloat16)
+        out = []
+        for k in nearest_first(NY):
+            to = lax.rem(y + k, NY)
+            out.append((k, copy(c, 3 + k, ys.at[c, to], yr.at[c, k - 1], place(to, x, z))))
+            out[-1][1].start()
+        return out
+
+    def send_z(c, before):
+        total = yown[c, y]
+        for k, one in before:
+            one.wait_recv()
+            total += yr[c, k - 1].astype(jnp.float32)[:span]
+        total = jnp.concatenate(
+            [total, jnp.zeros((pad - span, LANES), jnp.float32)], axis=0
+        ).astype(jnp.bfloat16)
+        line = lax.broadcasted_iota(jnp.int32, (NZ * tile, pad), 0)
+        wanted = lax.div(line, tile) * rows + lax.rem(line, tile)
+        column = lax.broadcasted_iota(jnp.int32, (NZ * tile, pad), 1)
+        spread = ((wanted == column) & (lax.rem(line, tile) < rows)).astype(jnp.bfloat16)
+        placed = jnp.dot(spread, total, preferred_element_type=jnp.float32)
+        zs[c] = placed.astype(jnp.bfloat16).reshape(NZ, tile, LANES)
+        out = []
+        for k in nearest_first(NZ):
+            to = lax.rem(z + k, NZ)
+            out.append((k, copy(c, 3 + NY - 1 + k, zs.at[c, to], zr.at[c, k - 1], place(y, x, to))))
+            out[-1][1].start()
+        return out
+
+    def finish(c, before):
+        start, _, width = chunks[c]
+        total = zs[c, z].astype(jnp.float32)
+        for k, one in before:
+            one.wait_recv()
+            total += zr[c, k - 1].astype(jnp.float32)
+        out_ref[:, start : start + width] = total[:rows, :width]
+
+    order = range(len(chunks))
+    stage1 = [first_x(c) for c in order]
+    stage2 = [second_x(c, stage1[c]) for c in order]
+    stage3 = [send_y(c, stage2[c]) for c in order]
+    stage4 = [send_z(c, stage3[c]) for c in order]
+    for c in order:
+        finish(c, stage4[c])
+    for c in order:
+        for one in stage1[c] + stage2[c]:
+            one.wait_send()
+        for _, one in stage3[c] + stage4[c]:
+            one.wait_send()
+
+
+def reduce_grad(st, upstream, rows):
+    tile = round_up(rows, 16)
+    pad = round_up(NZ * rows, 16)
+    full = st.shape[1]
+    n = 3
+    bf = jnp.bfloat16
+    slots = 4 + NY - 1 + NZ - 1
+    return pl.pallas_call(
+        grad_kernel,
+        out_shape=jax.ShapeDtypeStruct((rows, upstream.shape[1]), jnp.float32),
+        in_specs=[pl.BlockSpec(memory_space=pltpu.VMEM)] * 2,
+        out_specs=pl.BlockSpec(memory_space=pltpu.VMEM),
+        scratch_shapes=[
+            pltpu.VMEM((n, full, LANES), bf),
+            pltpu.VMEM((n, full, LANES), bf),
+            pltpu.VMEM((n, 2, full, LANES), bf),
+            pltpu.VMEM((n, 2, full, LANES), bf),
+            pltpu.VMEM((n, full, LANES), jnp.float32),
+            pltpu.VMEM((n, NY, pad, LANES), bf),
+            pltpu.VMEM((n, NY - 1, pad, LANES), bf),
+            pltpu.VMEM((n, NY, NZ * rows, LANES), jnp.float32),
+            pltpu.VMEM((n, NZ, tile, LANES), bf),
+            pltpu.VMEM((n, NZ - 1, tile, LANES), bf),
+            pltpu.SemaphoreType.DMA((n, slots)),
+            pltpu.SemaphoreType.DMA((n, slots)),
+        ],
+        compiler_params=pltpu.CompilerParams(
+            collective_id=0, has_side_effects=True, vmem_limit_bytes=40 << 20
+        ),
+    )(st, upstream)
 
 
 def local(
@@ -47,14 +246,10 @@
             - (cosine / (predict_norm * predict_norm))[:, None] * predicted
         )
     ).astype(jnp.bfloat16)
-    return lax.psum_scatter(
-        lax.dot_general(
-            student_feat, upstream, (((0,), (0,)), ((), ())), preferred_element_type=jnp.float32
-        ),
-        "dp",
-        scatter_dimension=0,
-        tiled=True,
-    )
+    rows = student_feat.shape[1] // dp_devices
+    st = student_feat.T.reshape(NY, NX, NZ * rows, row_count)
+    st = jnp.swapaxes(st, 0, 1).reshape(NX, NY * NZ * rows, row_count)
+    return reduce_grad(st, upstream, rows)
 
 
 def solution(mesh):

time: 1650 us -> 154 us (0.09)
  the two profiles are of different devices: /device:TPU:32 before, /device:TPU:16 now
where the time goes in v1:
time: 154 us
  waiting for transfers between devices  52.3 us (34%)
  Pallas kernels  26.2 us (17%)
  blocking collectives  23.7 us (15%)
  starting transfers between devices  20.8 us (14%)
  between operations  13.5 us (9%)
  matrix products  9.22 us (6%)
  other arithmetic  4.77 us (3%)
  local copies, waits for them, and re-layouts  3.42 us (2%)
    reduce_scatter x1, waiting for transfers between devices, local(): lax.psum_scatter(partial_value, 'tensor', scatter_dimension=1, tiled=True)  37.5 us
    pallas_call x1, Pallas kernels, reduce_grad(): pl.pallas_call(grad_kernel, out_shape=jax.ShapeDtypeStruct((rows, upstrea...  26.2 us
    all_to_all x1, starting transfers between devices, local(): lax.all_to_all(feature[arrival], 'dp', split_axis=0, concat_axis=0, tiled...  20.8 us
    all_to_all x1, waiting for transfers between devices, local(): lax.all_to_all(feature[arrival], 'dp', split_axis=0, concat_axis=0, tiled...  14.8 us
    all_gather x1, blocking collectives, local(): gathered = lax.all_gather(teacher_in, 'tensor', axis=1, tiled=True)  13.2 us
    psum x1, blocking collectives, local(): lax.psum((jnp.sum(target_wide * predicted, axis=1), jnp.sum(target_wide *...  10.5 us
    dot_general x1, matrix products, local(): jnp.dot(hidden, fc2_weight, preferred_element_type=jnp.float32)  8.84 us
  transfers between devices with their start and end apart: 2, of which 2 were waited for; matrix products, arithmetic and copies ran while one was open for 2% of the time, Pallas kernels for 0%

profile of v1, /device:TPU:16, one launch (start us, length us, event | category | flops | bytes accessed | tf_op | source)
XLA Modules:
  0.0 154.0 jit_solution(2783848099819664387)
XLA Ops:
  6.5 0.0 copy-start
  6.5 0.0 reduce-scatter.2.cloned.1.call-start
  6.5 13.2 %all_gather.3 = bf16[128,1920]{0,1:T(8,128)(2,1)S(1)} all-gather(bf16[128,320]{0,1:T(8,128)(2,1)} %param.8), channel_id=1, replica_groups=mesh['dp'=128,'tensor'=6] {'tensor'}, dimensions={1}, use_global_device_ids=true | all-gather | bytes 573440 | tf_op jit(solution)/shard_map/all_gather | solution.py:215
  19.8 0.3 fusion
  20.0 0.0 copy-start.1
  20.1 0.0 copy-start.4
  20.1 0.0 copy-start.2
  20.1 0.0 copy-start.3
  20.1 8.8 %fusion.18 = f32[128,1920]{0,1:T(8,128)} fusion(bf16[1280,1920]{1,0:T(8,128)(2,1)} %param.11, bf16[1920,1280]{1,0:T(8,128)(2,1)} %param.10, bf16[128,1920]{0,1:T(8,128)(2,1)S(1)} %all_gather.3, f32[1920]{0:T(1024)} %param.9, f32[128]{0:T(128)S(1)} %add_rsqrt_fusion), kind=kOutput, calls=%fused_computation.26 | convolution fusion | flops 1269923840 | bytes 11313152 | tf_op jit(solution)/shard_map/dot_general | solution.py:223
  28.9 0.0 reduce-scatter.2.cloned.1.call-update
  29.0 0.0 copy-done.1
  29.0 0.2 copy.18
  29.2 0.0 copy-done.4
  29.2 2.5 %sort.17 = (s32[128]{0:T(128)}, s32[128]{0:T(128)S(1)}) sort(s32[128]{0:T(128)S(1)} %iota_add_fusion, s32[128]{0:T(128)S(1)} %iota.8), dimensions={0}, to_apply=%region_2.3 | sort | flops 896 | bytes 2048 | tf_op jit(solution)/shard_map/jit(argsort)/sort | solution.py:214
  31.8 37.5 %reduce-scatter.2.cloned.1.call-done = f32[128,320]{0,1:T(8,128)} async-done(((f32[128,1920]{0,1:T(8,128)}), f32[128,320]{0,1:T(8,128)}) %reduce-scatter.2.cloned.1.call-update) | async-done | bytes 163856 | tf_op jit(solution)/shard_map/reduce_scatter | solution.py:224
  69.3 0.0 copy-done.2
  69.3 0.0 copy-done.3
  69.3 1.0 add_convert_fusion
  70.3 0.1 copy.20
  70.4 0.9 gather_fusion
  71.3 0.5 broadcast.34
  71.8 0.7 reduce
  72.5 0.7 reshape.34
  73.2 20.8 %all-to-all-start = ((bf16[128,2,160]{2,1,0:T(2,128)(2,1)}), bf16[128,2,160]{2,1,0:T(2,128)(2,1)S(1)}, u32[]{:S(2)}, u32[]{:S(2)}) async-start(bf16[128,2,160]{2,1,0:T(2,128)(2,1)} %reshape.34), calls=%async_computation.1 | async-start | bytes 262144 | tf_op jit(solution)/shard_map/all_to_all | solution.py:226
  94.0 0.0 copy-done
  94.0 0.4 multiply_reduce_fusion
  94.4 0.1 copy.23
  94.6 14.8 %all-to-all-done = bf16[128,2,160]{2,1,0:T(2,128)(2,1)S(1)} async-done(((bf16[128,2,160]{2,1,0:T(2,128)(2,1)}), bf16[128,2,160]{2,1,0:T(2,128)(2,1)S(1)}, u32[]{:S(2)}, u32[]{:S(2)}) %all-to-all-start) | async-done | bytes 81952 | tf_op jit(solution)/shard_map/all_to_all | solution.py:226
  109.4 0.2 reshape.35
  109.5 0.1 fusion.54
  109.6 10.5 %all-reduce = (f32[128]{0:T(128)S(1)}, f32[128]{0:T(128)S(1)}, f32[128]{0:T(128)S(1)}) all-reduce(f32[128]{0:T(128)S(1)} %get-tuple-element.8, f32[128]{0:T(128)S(1)} %get-tuple-element.14, f32[128]{0:T(128)S(1)} %get-tuple-element.7), channel_id=1, replica_groups=mesh['dp'=128,'tensor'=6] {'tensor'}, use_global_device_ids=true, to_apply=%region_8.9 | all-reduce | flops 384 | bytes 3072 | tf_op jit(solution)/shard_map/psum | solution.py:229
  120.2 0.1 fusion.57.u_ref
  120.3 26.2 %shard_map.82 = f32[10,320]{1,0:T(8,128)S(1)} custom-call(bf16[4,320,128]{2,1,0:T(8,128)(2,1)S(1)} %bitcast.16, bf16[128,320]{1,0:T(8,128)(2,1)S(1)} %fusion.57.u_ref), custom_call_target="tpu_custom_call" | custom-call | tf_op jit(solution)/shard_map/pallas_call | solution.py:183
  146.5 0.6 copy.30
  (7 shorter events, 0.1 us)
Async XLA Ops:
  6.5 87.5 %copy-start = (bf16[1280,320]{0,1:T(8,128)(2,1)S(1)}, bf16[1280,320]{0,1:T(8,128)(2,1)}, u32[]{:S(2)}) copy-start(bf16[1280,320]{0,1:T(8,128)(2,1)} %param.15) | copy-start | bytes 2457604
  6.5 62.7 %reduce-scatter.2.cloned.1.call-start = ((), (), s32[]{:S(2)}) async-start(), calls=%async_computation.2 | async-start | bytes 1146880 | tf_op jit(solution)/shard_map/reduce_scatter | solution.py:224
  20.0 8.9 %copy-start.1 = (bf16[128,1280]{1,0:T(8,128)(2,1)S(1)}, bf16[128,1280]{1,0:T(8,128)(2,1)}, u32[]{:S(2)}) copy-start(bf16[128,1280]{1,0:T(8,128)(2,1)} %param.14) | copy-start | bytes 983044
  20.1 9.1 %copy-start.4 = (s32[128]{0:T(128)S(1)}, s32[128]{0:T(128)}, u32[]{:S(2)}) copy-start(s32[128]{0:T(128)} %param.13) | copy-start | bytes 1540
  20.1 49.2 %copy-start.2 = (bf16[128,320]{0,1:T(8,128)(2,1)S(1)}, bf16[128,320]{0,1:T(8,128)(2,1)}, u32[]{:S(2)}) copy-start(bf16[128,320]{0,1:T(8,128)(2,1)} %param.8) | copy-start | bytes 245764
  20.1 49.2 %copy-start.3 = (f32[320]{0:T(512)S(1)}, f32[320]{0:T(512)}, u32[]{:S(2)}) copy-start(f32[320]{0:T(512)} %param.12) | copy-start | bytes 3844
  73.2 36.1 %all-to-all-start = ((bf16[128,2,160]{2,1,0:T(2,128)(2,1)}), bf16[128,2,160]{2,1,0:T(2,128)(2,1)S(1)}, u32[]{:S(2)}, u32[]{:S(2)}) async-start(bf16[128,2,160]{2,1,0:T(2,128)(2,1)} %reshape.34), calls=%async_computation.1 | async-start | bytes 262144 | tf_op jit(solution)/shard_map/all_to_all | solution.py:226
Sparse Core Ops, SparseCore 0:
  29.1 40.1 reduce-scatter.1

commit v2 on v1

--- a/solution.py
+++ b/solution.py
@@ -22,7 +22,7 @@
 
 
 def dp_peers(y, x, z):
-    peers = [place(y, lax.rem(x + k, NX), z) for k in (1, NX - 1)]
+    peers = [place(y, lax.rem(x + k, NX), z) for k in range(1, NX)]
     peers += [place(lax.rem(y + k, NY), x, z) for k in range(1, NY)]
     peers += [place(y, x, lax.rem(z + k, NZ)) for k in range(1, NZ)]
     return peers
@@ -35,12 +35,41 @@
     return order
 
 
-def grad_kernel(st_ref, u_ref, out_ref, s1, r1, s2, r2, own, ys, yr, yown, zs, zr, send, recv):
+def erf_gelu(value):
+    return 0.5 * value * (1.0 + lax.erf(value * (1.0 / math.sqrt(2.0))))
+
+
+def one_hot(rows, columns, source):
+    line = lax.broadcasted_iota(jnp.int32, (rows, columns), 0)
+    column = lax.broadcasted_iota(jnp.int32, (rows, columns), 1)
+    return (source(line) == column).astype(jnp.bfloat16)
+
+
+def select_rows(matrix, value):
+    return jnp.dot(matrix, value, preferred_element_type=jnp.float32)
+
+
+def kernel(
+    scale, x_hbm, gain_ref, fc1_hbm, fc2_hbm, ls_ref, route_ref, stud_hbm, aw_hbm, out_ref,
+    fc1, fc2, aw, xg, acc, mine, pair_s, pair_r, chip_s, chip_r,
+    b1, b1s, b2, b2s, sfull, turned, st_ref, pred_ref, stat_s, stat_r, u_ref,
+    s1, r1, s2, r2, own, ys, yr, yown, zs, zr,
+    send, recv, tsend, trecv, local_sem,
+):
+    bf, f32 = jnp.bfloat16, jnp.float32
     me = lax.axis_index("dp")
     z = lax.rem(me, NZ)
     x = lax.rem(lax.div(me, NZ), NX)
     y = lax.div(me, NZ * NX)
     right, left, across = (lax.rem(x + k, NX) for k in (1, 3, 2))
+    t = lax.axis_index("tensor")
+    chip, core = lax.div(t, 2), lax.rem(t, 2)
+    twin = chip * 2 + 1 - core
+    near = jnp.where(chip == 1, 0, 1)
+    far = jnp.where(chip == 2, 0, 2)
+
+    tokens, width = xg.shape[1:]
+    half = stud_hbm.shape[1] // 2
     rows = out_ref.shape[0]
     span = NZ * rows
     pad = round_up(span, 16)
@@ -48,19 +77,211 @@
     full = NY * span
     chunks = [(0, full, 128), (128, full, 128), (256, full // 2, 64)]
 
+    loads = []
+
+    def load(slot, src, dst):
+        one = pltpu.make_async_copy(src, dst, local_sem.at[slot])
+        one.start()
+        return one
+
+    load_x = load(0, x_hbm, xg.at[t])
+    lanes = pl.ds(pl.multiple_of(core * half, half), half)
+    block_rows = NX * NZ
+
+    def student_block(to):
+        return stud_hbm.at[pl.ds(pl.multiple_of(to * block_rows, block_rows), block_rows), lanes]
+
+    load_stud = load(1, student_block(y), b1.at[y])
+    load_fc1 = load(2, fc1_hbm, fc1)
+    load_fc2 = [load(3 + q, fc2_hbm.at[:, pl.ds(q * 2 * width, 2 * width)], fc2.at[q]) for q in range(3)]
+    load_aw = load(6, aw_hbm, aw)
+
     barrier = pltpu.get_barrier_semaphore()
-    peers = dp_peers(y, x, z)
+    peers = [{"tensor": lax.rem(t + k, 6)} for k in range(1, 6)]
+    peers += [{"dp": peer} for peer in dp_peers(y, x, z)]
     for peer in peers:
-        pl.semaphore_signal(barrier, inc=1, device_id={"dp": peer}, device_id_type=MESH)
+        pl.semaphore_signal(barrier, inc=1, device_id=peer, device_id_type=MESH)
     pl.semaphore_wait(barrier, len(peers))
+
+    sent = []
+
+    def remote(slot, src, dst, peer, arrive=None):
+        arrive = slot if arrive is None else arrive
+        return pltpu.make_async_remote_copy(
+            src_ref=src, dst_ref=dst, send_sem=tsend.at[slot], recv_sem=trecv.at[arrive],
+            device_id=peer, device_id_type=MESH,
+        )
+
+    def begin(one):
+        one.start()
+        sent.append(one)
+        return one
+
+    load_x.wait()
+    for slot, to in ((0, far), (1, near)):
+        begin(remote(slot, xg.at[t], xg.at[t], {"tensor": to * 2 + core}, chip))
+    from_twin = begin(remote(6, xg.at[t], xg.at[t], {"tensor": twin}))
+
+    stage_y = []
+    for k in nearest_first(NY):
+        to = lax.rem(y + k, NY)
+        stage_y.append(begin(remote(
+            19 + k, student_block(to), b1.at[y], {"dp": place(to, x, z)}
+        )))
+
+    def arrived_y(k):
+        origin = lax.rem(y + NY - k, NY)
+        return remote(19 + k, b1.at[origin], b1.at[origin], {"dp": place(origin, x, z)})
+
+    squares = []
+
+    def accumulate(source):
+        value = xg[source].astype(f32)
+        squares.append(jnp.sum(value * value, axis=1, keepdims=True))
+        part = jnp.dot(
+            (value * gain_ref[source]).astype(bf), fc1[source], preferred_element_type=f32
+        )
+        if len(squares) == 1:
+            acc[...] = part
+        else:
+            acc[...] += part
+
+    def gathered(source, base, origin):
+        return remote(base, xg.at[source], xg.at[source], {"tensor": twin}, base + origin)
+
+    def pass_on(slot, origin):
+        source = origin * 2 + core
+        gathered(source, 0, origin).wait_recv()
+        begin(remote(slot, xg.at[source], xg.at[source], {"tensor": twin}, 3 + origin))
+
+    load_fc1.wait()
+    accumulate(t)
+    pass_on(2, near)
+    from_twin.wait_recv()
+    accumulate(twin)
+    pass_on(3, far)
+    accumulate(near * 2 + core)
+
+    load_stud.wait()
+    for k in range(1, NY):
+        arrived_y(k).wait_recv()
+    count = NY * NX * NZ
+    by_x = one_hot(count, count, lambda o: (
+        lax.rem(o, NY) * (NX * NZ) + lax.div(o, NY * NZ) * NZ + lax.rem(lax.div(o, NY), NZ)
+    ))
+    b1s[...] = select_rows(by_x, b1[...].reshape(count, half)).astype(bf).reshape(b1s.shape)
+    b2[x] = b1s[x]
+    for k in nearest_first(NX):
+        to = lax.rem(x + k, NX)
+        begin(remote(29 + k, b1s.at[to], b2.at[x], {"dp": place(y, to, z)}))
+
+    accumulate(far * 2 + core)
+    gathered(near * 2 + 1 - core, 3, near).wait_recv()
+    accumulate(near * 2 + 1 - core)
+
+    for k in range(1, NX):
+        origin = lax.rem(x + NX - k, NX)
+        remote(29 + k, b2.at[origin], b2.at[origin], {"dp": place(y, origin, z)}).wait_recv()
+    by_z = one_hot(count, count, lambda o: (
+        lax.rem(lax.div(o, NY), NX) * (NZ * NY) + lax.div(o, NY * NX) * NY + lax.rem(o, NY)
+    ))
+    b2s[...] = select_rows(by_z, b2[...].reshape(count, half)).astype(bf).reshape(b2s.shape)
+    sfull[core, z] = b2s[z]
+    for k in nearest_first(NZ):
+        to = lax.rem(z + k, NZ)
+        begin(remote(32 + k, b2s.at[to], sfull.at[core, z], {"dp": place(y, x, to)}))
+
+    gathered(far * 2 + 1 - core, 3, far).wait_recv()
+    accumulate(far * 2 + 1 - core)
+
+    factor = lax.rsqrt(sum(squares) * (1.0 / (6 * width)) + 1e-06)
+    hidden = erf_gelu(acc[...] * factor).astype(bf)
+
+    pairs = []
+    for one in load_fc2:
+        one.wait()
+    for slot, q in ((7, far), (8, near), (9, chip)):
+        part = jnp.dot(hidden, fc2[q], preferred_element_type=f32)
+        low, high = part[:, :width], part[:, width:]
+        pair_s[slot - 7] = jnp.where(core == 0, high, low).astype(bf)
+        pairs.append(begin(remote(slot, pair_s.at[slot - 7], pair_r.at[slot - 7], {"tensor": twin})))
+        mine[slot - 7] = jnp.where(core == 0, low, high)
+    for i, q in enumerate((far, near)):
+        pairs[i].wait_recv()
+        chip_s[i] = (mine[i] + pair_r[i].astype(f32)).astype(bf)
+        begin(remote(10 + i, chip_s.at[i], chip_r.at[chip], {"tensor": q * 2 + core}, 10 + chip))
+
+    for k in range(1, NZ):
+        origin = lax.rem(z + NZ - k, NZ)
+        remote(
+            32 + k, sfull.at[core, origin], sfull.at[core, origin], {"dp": place(y, x, origin)}
+        ).wait_recv()
+    twin_half = begin(remote(13, sfull.at[core], sfull.at[core], {"tensor": twin}))
+    slot_of = lax.broadcasted_iota(jnp.int32, (count, tokens), 0)
+    owner = (lax.rem(slot_of, NY) * NX + lax.rem(lax.div(slot_of, NY), NX)) * NZ + lax.div(
+        slot_of, NY * NX
+    )
+    chosen = owner == route_ref[...]
+    match = chosen.astype(bf)
+    match_t = jnp.transpose(chosen.astype(f32)).astype(bf)
+    load_aw.wait()
+
+    def student(side):
+        value = sfull[side].reshape(count, half)
+        ordered = select_rows(match_t, value).astype(bf)
+        turned[side] = lax.dot_general(
+            value, match, (((0,), (0,)), ((), ())), preferred_element_type=f32
+        )
+        return jnp.dot(ordered, aw[side], preferred_element_type=f32)
+
+    pred_ref[...] = student(core)
+    remote(13, sfull.at[1 - core], sfull.at[1 - core], {"tensor": twin}).wait_recv()
+    pred_ref[...] += student(1 - core)
+    both = turned[...].reshape(NY, NX, span, tokens)
+    for k in range(NX):
+        st_ref[k] = both[:, k].reshape(full, tokens).astype(bf)
+
+    predicted = pred_ref[...]
+    predict_sq = jnp.sum(predicted * predicted, axis=1, keepdims=True)
+    pairs[2].wait_recv()
+    mlp = mine[2] + pair_r[2].astype(f32)
+    for q in (near, far):
+        remote(10, chip_r.at[q], chip_r.at[q], {"tensor": twin}, 10 + q).wait_recv()
+        mlp += chip_r[q].astype(f32)
+    target = (xg[t].astype(f32) + ls_ref[...] * mlp).astype(bf).astype(f32)
+
+    lane = lax.broadcasted_iota(jnp.int32, (tokens, LANES), 1)
+    sums = jnp.where(lane == 0, jnp.sum(target * predicted, axis=1, keepdims=True), 0.0)
+    sums = jnp.where(lane == 1, jnp.sum(target * target, axis=1, keepdims=True), sums)
+    sums = jnp.where(lane == 2, predict_sq, sums)
+    stat_s[...] = jnp.transpose(sums)[:8]
+    shared = [
+        begin(remote(13 + k, stat_s, stat_r.at[k - 1], {"tensor": lax.rem(t + k, 6)}))
+        for k in range(1, 6)
+    ]
+    total = stat_s[...]
+    for k, one in enumerate(shared):
+        one.wait_recv()
+        total += stat_r[k]
+    total = jnp.concatenate([total, jnp.zeros((LANES - 8, tokens), f32)], axis=0)
+    columns = jnp.transpose(total)
+    agreement, target_sq, predict_sq = (columns[:, i : i + 1] for i in range(3))
+    target_norm = jnp.sqrt(target_sq + 1e-06)
+    predict_norm = jnp.sqrt(predict_sq + 1e-06)
+    cosine = agreement / (target_norm * predict_norm)
+    u_ref[...] = (
+        -scale
+        * (
+            target * (1.0 / (target_norm * predict_norm))
+            - (cosine / (predict_norm * predict_norm)) * predicted
+        )
+    ).astype(bf)
 
     def copy(c, slot, src, dst, peer):
         return pltpu.make_async_remote_copy(
             src_ref=src, dst_ref=dst, send_sem=send.at[c, slot], recv_sem=recv.at[c, slot],
             device_id={"dp": peer}, device_id_type=MESH,
         )
-
-    started = []
 
     def product(c, block):
         start, height, width = chunks[c]
@@ -172,84 +393,91 @@
         for _, one in stage3[c] + stage4[c]:
             one.wait_send()
 
-
-def reduce_grad(st, upstream, rows):
+    for one in sent:
+        one.wait_send()
+
+
+def fused(scale, rows, x, gain, fc1, fc2, ls, route, stud, aw):
+    bf, f32 = jnp.bfloat16, jnp.float32
+    tokens, width = x.shape
+    hidden = fc2.shape[0]
+    half = stud.shape[1] // 2
+    count = NY * NX * NZ
     tile = round_up(rows, 16)
     pad = round_up(NZ * rows, 16)
-    full = st.shape[1]
+    full = NY * NZ * rows
     n = 3
-    bf = jnp.bfloat16
     slots = 4 + NY - 1 + NZ - 1
+    vmem = pl.BlockSpec(memory_space=pltpu.VMEM)
+    hbm = pl.BlockSpec(memory_space=pl.ANY)
     return pl.pallas_call(
-        grad_kernel,
-        out_shape=jax.ShapeDtypeStruct((rows, upstream.shape[1]), jnp.float32),
-        in_specs=[pl.BlockSpec(memory_space=pltpu.VMEM)] * 2,
-        out_specs=pl.BlockSpec(memory_space=pltpu.VMEM),
+        functools.partial(kernel, scale),
+        out_shape=jax.ShapeDtypeStruct((rows, width), f32),
+        in_specs=[hbm, vmem, hbm, hbm, vmem, vmem, hbm, hbm],
+        out_specs=vmem,
         scratch_shapes=[
+            pltpu.VMEM((6, width, hidden), bf),
+            pltpu.VMEM((3, hidden, 2 * width), bf),
+            pltpu.VMEM((2, half, width), bf),
+            pltpu.VMEM((6, tokens, width), bf),
+            pltpu.VMEM((tokens, hidden), f32),
+            pltpu.VMEM((3, tokens, width), f32),
+            pltpu.VMEM((3, tokens, width), bf),
+            pltpu.VMEM((3, tokens, width), bf),
+            pltpu.VMEM((2, tokens, width), bf),
+            pltpu.VMEM((3, tokens, width), bf),
+            pltpu.VMEM((NY, NX * NZ, half), bf),
+            pltpu.VMEM((NX, NZ * NY, half), bf),
+            pltpu.VMEM((NX, NZ * NY, half), bf),
+            pltpu.VMEM((NZ, NX * NY, half), bf),
+            pltpu.VMEM((2, NZ, NX * NY, half), bf),
+            pltpu.VMEM((2, half, tokens), f32),
+            pltpu.VMEM((NX, full, tokens), bf),
+            pltpu.VMEM((tokens, width), f32),
+            pltpu.VMEM((8, tokens), f32),
+            pltpu.VMEM((5, 8, tokens), f32),
+            pltpu.VMEM((tokens, width), bf),
             pltpu.VMEM((n, full, LANES), bf),
             pltpu.VMEM((n, full, LANES), bf),
             pltpu.VMEM((n, 2, full, LANES), bf),
             pltpu.VMEM((n, 2, full, LANES), bf),
-            pltpu.VMEM((n, full, LANES), jnp.float32),
+            pltpu.VMEM((n, full, LANES), f32),
             pltpu.VMEM((n, NY, pad, LANES), bf),
             pltpu.VMEM((n, NY - 1, pad, LANES), bf),
-            pltpu.VMEM((n, NY, NZ * rows, LANES), jnp.float32),
+            pltpu.VMEM((n, NY, NZ * rows, LANES), f32),
             pltpu.VMEM((n, NZ, tile, LANES), bf),
             pltpu.VMEM((n, NZ - 1, tile, LANES), bf),
             pltpu.SemaphoreType.DMA((n, slots)),
             pltpu.SemaphoreType.DMA((n, slots)),
+            pltpu.SemaphoreType.DMA((40,)),
+            pltpu.SemaphoreType.DMA((40,)),
+            pltpu.SemaphoreType.DMA((8,)),
         ],
         compiler_params=pltpu.CompilerParams(
-            collective_id=0, has_side_effects=True, vmem_limit_bytes=40 << 20
+            collective_id=0, has_side_effects=True, vmem_limit_bytes=48 << 20
         ),
-    )(st, upstream)
+    )(x, gain, fc1, fc2, ls, route, stud, aw)
 
 
 def local(
     teacher_in, norm_gain, fc1_weight, fc2_weight, layer_scale, route, student_feat, adaptor_weight
 ):
-    row_count = teacher_in.shape[0]
-    dp_devices = lax.axis_size("dp")
-    sort_keys = route * row_count + jnp.arange(row_count, dtype=jnp.int32)
-    arrival = jnp.argsort(sort_keys)
-    gathered = lax.all_gather(teacher_in, "tensor", axis=1, tiled=True)
-    widened = gathered.astype(jnp.float32)
-    normed = (
-        widened * lax.rsqrt(jnp.mean(widened * widened, axis=1, keepdims=True) + 1e-06) * norm_gain
-    ).astype(jnp.bfloat16)
-    hidden = jax.nn.gelu(
-        jnp.dot(normed, fc1_weight, preferred_element_type=jnp.float32), approximate=False
-    ).astype(jnp.bfloat16)
-    partial_value = jnp.dot(hidden, fc2_weight, preferred_element_type=jnp.float32)
-    mlp_output = lax.psum_scatter(partial_value, "tensor", scatter_dimension=1, tiled=True)
-    feature = (teacher_in.astype(jnp.float32) + layer_scale * mlp_output).astype(jnp.bfloat16)
-    target = lax.all_to_all(feature[arrival], "dp", split_axis=0, concat_axis=0, tiled=True)
-    predicted = jnp.dot(student_feat, adaptor_weight, preferred_element_type=jnp.float32)
-    target_wide = target.astype(jnp.float32)
-    agreement, target_sq, predict_sq = lax.psum(
-        (
-            jnp.sum(target_wide * predicted, axis=1),
-            jnp.sum(target_wide * target_wide, axis=1),
-            jnp.sum(predicted * predicted, axis=1),
-        ),
-        "tensor",
+    tokens, width = teacher_in.shape
+    features = student_feat.shape[1]
+    dp_devices, parts = lax.axis_size("dp"), lax.axis_size("tensor")
+    scale = width * parts / math.sqrt(tokens * dp_devices)
+    return fused(
+        scale,
+        features // dp_devices,
+        teacher_in,
+        norm_gain.reshape(parts, 1, width),
+        fc1_weight.reshape(parts, width, fc1_weight.shape[1]),
+        fc2_weight,
+        layer_scale.reshape(1, width),
+        route.reshape(1, tokens),
+        student_feat,
+        adaptor_weight.reshape(2, features // 2, width),
     )
-    target_norm = jnp.sqrt(target_sq + 1e-06)
-    predict_norm = jnp.sqrt(predict_sq + 1e-06)
-    cosine = agreement / (target_norm * predict_norm)
-    teacher_width = adaptor_weight.shape[1] * lax.axis_size("tensor")
-    loss_scale = teacher_width / math.sqrt(row_count * dp_devices)
-    upstream = (
-        -loss_scale
-        * (
-            target_wide / (target_norm * predict_norm)[:, None]
-            - (cosine / (predict_norm * predict_norm))[:, None] * predicted
-        )
-    ).astype(jnp.bfloat16)
-    rows = student_feat.shape[1] // dp_devices
-    st = student_feat.T.reshape(NY, NX, NZ * rows, row_count)
-    st = jnp.swapaxes(st, 0, 1).reshape(NX, NY * NZ * rows, row_count)
-    return reduce_grad(st, upstream, rows)
 
 
 def solution(mesh):

time: 154 us -> 74.9 us (0.49)
  the two profiles are of different devices: /device:TPU:16 before, /device:TPU:8 now
where the time goes in v2:
time: 74.9 us; the launch traced here: 74.6 us
  Pallas kernels  68.4 us (91%)
  local copies, waits for them, and re-layouts  6.24 us (8%)
    pallas_call x1, Pallas kernels, fused(): pl.pallas_call(functools.partial(kernel, scale), out_shape=jax.ShapeDtype...  68.4 us
    unnamed x7, local copies, waits for them, and re-layouts  4.79 us

profile of v2, /device:TPU:8, one launch (start us, length us, event | category | flops | bytes accessed | tf_op | source)
XLA Modules:
  0.0 74.6 jit_solution(14530388293578570914)
XLA Ops:
  0.0 0.7 reshape.17.ls_ref
  0.7 0.8 %reshape.15.gain_ref = f32[6,1,320]{2,1,0:T(1,128)S(1)} reshape(f32[1920]{0:T(1024)} %param.9) | data formatting | bytes 15360 | tf_op jit(solution)/shard_map/reshape | solution.py:473
  1.5 1.0 %copy.10.x_hbm = bf16[128,320]{1,0:T(8,128)(2,1)S(1)} copy(bf16[128,320]{0,1:T(8,128)(2,1)} %param.8) | data formatting | bytes 163840 | tf_op args[0]
  2.5 1.6 %copy.9 = bf16[1280,320]{1,0:T(8,128)(2,1)S(1)} copy(bf16[1280,320]{0,1:T(8,128)(2,1)} %param.15) | data formatting | bytes 1638400 | tf_op args[7]
  4.0 0.0 copy-start
  4.0 1.0 %copy-done = bf16[128,1280]{1,0:T(8,128)(2,1)S(1)} copy-done((bf16[128,1280]{1,0:T(8,128)(2,1)S(1)}, bf16[128,1280]{1,0:T(8,128)(2,1)}, u32[]{:S(2)}) %copy-start) | copy-done | bytes 327704
  5.0 0.0 copy-start.1
  5.0 0.7 copy-done.1
  5.7 68.4 %shard_map.82 = f32[10,320]{1,0:T(8,128)S(1)} custom-call(bf16[128,320]{1,0:T(8,128)(2,1)S(1)} %copy.10.x_hbm, f32[6,1,320]{2,1,0:T(1,128)S(1)} %reshape.15.gain_ref, bf16[6,320,1280]{2,1,0:T(8,128)(2,1)} %bitcast.5, bf16[1280,1920]{1,0:T(8,128)(2,1)} %fc2_hbm.1, f32[1,320]{1,0:T(1,128)S(1)} %reshape.17.ls_ref, s32[1,128]{1,0:T(1,128)S(1)} %bitcast.4, ...), custom_call_target="tpu_custom_call" | custom-call | tf_op jit(solution)/shard_map/pallas_call | solution.py:413
  74.0 0.6 copy.12
Async XLA Ops:
  4.0 1.0 %copy-start = (bf16[128,1280]{1,0:T(8,128)(2,1)S(1)}, bf16[128,1280]{1,0:T(8,128)(2,1)}, u32[]{:S(2)}) copy-start(bf16[128,1280]{1,0:T(8,128)(2,1)} %stud_hbm.1) | copy-start | bytes 983044
  5.0 0.7 copy-start.1
